TPU v7x, 32 devices: a whole 2x2x4 slice. The times are simulated.
32 devices in a mesh: row: 4 (over y, x), col: 8 (over z, core).
Axes of the slice: x: 2, y: 2, z: 4, core: 2. Of those that a mesh axis runs over, the one named last changes fastest.
Arguments:
- features: bfloat16 [16384, 256], P(('col', 'row')), may hold values from -6 to 6
- weight: bfloat16 [256, 256], replicated, may hold values from -0.375 to 0.375
- adjacency: int32 [64, 16, 256, 256], P('row', 'col'), may hold values 0 or 1
- tile_cols: int32 [64, 16], P('row', 'col'), may hold values from 0 to 7
- tile_counts: int32 [64, 8], P('row', 'col'), may hold values from 0 to 2
- cotangent: bfloat16 [16384, 256], P(('row', 'col')), may hold values from -6 to 6
Outputs:
- output: bfloat16 [16384, 256], P(('row', 'col'))
- feature_grad: bfloat16 [16384, 256], P(('col', 'row'))
- weight_grad: float32 [256, 256], replicated
Inputs may be any that keep to these rules, and one draw needn't show every extreme that they name: `tile_counts`: slots of a block row at or after its count are not part of the graph.
All inputs are finite; a program needn't handle non-finite values. No bound on the sum of `adjacency` on one device may be relied on, other than what follows from the above.
Results may differ from a plain program's by a relative error of at most 0.0061.
Values may be sent and summed in bfloat16 or wider, within the bound.
A program may use at most 128 MiB of HBM per device.

v0:
```python
import math
import jax
import jax.numpy as jnp
from jax import lax
from jax.sharding import PartitionSpec as P


def shards(features, weight, adjacency, tile_cols, tile_counts, cotangent):
    block_rows = adjacency.shape[0]
    slot_count = adjacency.shape[1]
    tile_len = adjacency.shape[2]
    feat_width = features.shape[1]
    own_rows = features.shape[0]
    counts = tile_counts[:, 0]
    usable = jnp.arange(slot_count)[None, :] < counts[:, None]
    col_inputs = lax.all_gather(features, "row", axis=0, tiled=True)
    col_hidden = jnp.dot(col_inputs, weight, preferred_element_type=jnp.float32).astype(
        jnp.bfloat16
    )
    col_blocks = col_hidden.shape[0] // tile_len
    blocks = col_hidden.reshape(col_blocks, tile_len, feat_width)
    panels = jnp.take(blocks, tile_cols, axis=0)
    panels = jnp.where(usable[:, :, None, None], panels, jnp.zeros((), jnp.bfloat16))
    tile_bf = adjacency.astype(jnp.bfloat16)
    partial_value = jnp.einsum(
        "bkij,bkjf->bif", tile_bf, panels, preferred_element_type=jnp.float32
    )
    partial_value = partial_value.reshape(block_rows * tile_len, feat_width)
    row_sums = jnp.sum(adjacency, axis=3)
    row_degree = (
        jnp.sum(jnp.where(usable[:, :, None], row_sums, 0), axis=1).astype(jnp.float32).reshape(-1)
    )
    degree = lax.psum_scatter(row_degree, "col", scatter_dimension=0, tiled=True)
    summed = lax.psum_scatter(partial_value, "col", scatter_dimension=0, tiled=True)
    inv_root = lax.rsqrt(jnp.float32(1.0) + degree)[:, None]
    preact = summed * inv_root
    output = jax.nn.silu(preact).astype(jnp.bfloat16)
    sigmoid_v = jax.nn.sigmoid(preact)
    grad_sum = (
        cotangent.astype(jnp.float32) * sigmoid_v * (1.0 + preact * (1.0 - sigmoid_v)) * inv_root
    ).astype(jnp.bfloat16)
    grad_slab = lax.all_gather(grad_sum, "col", axis=0, tiled=True).reshape(
        block_rows, tile_len, feat_width
    )
    contribs = jnp.einsum("bkij,bif->bkjf", tile_bf, grad_slab, preferred_element_type=jnp.float32)
    onehot = (
        (tile_cols[:, :, None] == jnp.arange(col_blocks)[None, None, :]) & usable[:, :, None]
    ).astype(jnp.float32)
    col_partial = jnp.einsum("bkc,bkjf->cjf", onehot, contribs, precision=lax.Precision.HIGHEST)
    col_partial = col_partial.reshape(col_blocks * tile_len, feat_width)
    node_grad = lax.psum_scatter(col_partial, "row", scatter_dimension=0, tiled=True).astype(
        jnp.bfloat16
    )
    feature_grad = jnp.dot(node_grad, weight.T, preferred_element_type=jnp.float32).astype(
        jnp.bfloat16
    )
    node_total = own_rows * lax.axis_size("row") * lax.axis_size("col")
    weight_terms = jnp.dot(features.T, node_grad, preferred_element_type=jnp.float32)
    weight_grad = lax.psum(weight_terms, ("row", "col")) * jnp.float32(1.0 / math.sqrt(node_total))
    return (output, feature_grad, weight_grad)


def solution(mesh):
    placed = (
        P(("col", "row"), None),
        P(),
        P("row", "col", None, None),
        P("row", "col"),
        P("row", "col"),
        P(("row", "col"), None),
    )
    return jax.shard_map(
        shards,
        mesh=mesh,
        in_specs=placed,
        out_specs=(P(("row", "col"), None), P(("col", "row"), None), P()),
        check_vma=False,
    )
```

profile of v0, /device:TPU:0, one launch (start us, length us, event | category | flops | bytes accessed | tf_op | source)
XLA Modules:
  0.0 333.3 jit_solution(11807054258820807927)
XLA Ops:
  7.2 0.0 copy-start
  7.2 0.0 all-gather.3.cloned.1.call-start
  7.2 0.7 all-gather.3.cloned.1.call-update
  7.9 0.0 reduce-scatter.3.cloned.1.call-start
  8.0 0.7 compare_and_fusion
  8.6 0.1 copy.42
  8.7 0.7 compare_select_fusion
  9.4 0.1 copy.43
  9.5 0.1 reshape.78
  9.6 0.7 iota_compare_fusion.1
  10.4 28.9 %all-gather.3.cloned.1.call-done = bf16[2048,256]{1,0:T(8,128)(2,1)} async-done(((bf16[512,256]{1,0:T(8,128)(2,1)}), bf16[2048,256]{1,0:T(8,128)(2,1)}) %all-gather.3.cloned.1.call-update) | async-done | bytes 1048592 | tf_op jit(solution)/shard_map/all_gather | solution.py:16
  39.2 0.0 copy-done
  39.2 1.6 convolution_convert_fusion
  40.9 2.8 gather_fusion
  43.7 7.9 %fusion = f32[16,256,256,1]{1,2,3,0:T(8,128)} fusion(bf16[16,2,256,256]{3,2,1,0:T(8,128)(2,1)} %bitcast.36, pred[16,2]{1,0:T(8,128)(4,1)S(1)} %copy.42, pred[16,2]{1,0:T(8,128)(4,1)S(1)} %iota_compare_fusion.1, s32[16,2,256,256]{3,2,1,0:T(8,128)} %param.8), kind=kOutput, calls=%fused_computation.1 | convolution fusion | flops 1080033280 | bytes 16777280 | tf_op jit(solution)/shard_map/bkij,bkjf->bif/dot_general | solution.py:25
  51.6 0.0 reduce-scatter.3.cloned.1.call-update
  51.6 0.0 all-gather.5.cloned.1.call-start
  51.7 0.0 copy-start.4
  51.7 0.0 copy-start.2
  51.7 4.6 %reduce_sum.18 = s32[16,2,256]{2,1,0:T(2,128)S(1)} reduce(s32[16,2,256,256]{3,2,1,0:T(8,128)} %param.8, s32[]{:T(128)} %constant.7.clone.1), dimensions={3}, to_apply=%region_1.2 | reduce | flops 2088960 | bytes 8421380 | tf_op jit(solution)/shard_map/reduce_sum | solution.py:29
  56.3 0.1 select_reduce_fusion
  56.4 0.0 copy-done.4
  56.5 0.6 dynamic-slice
  57.7 30.4 %all-reduce = f32[4096]{0:T(1024)S(1)} all-reduce(f32[4096]{0:T(1024)S(1)} %bitcast.40), channel_id=3, replica_groups=mesh['row'=4,'col'=8] {'col'}, use_global_device_ids=true, to_apply=%region_3.4.clone | all-reduce | flops 4096 | bytes 32768
  88.1 0.1 fusion.16
  88.2 14.2 %reduce-scatter.3.cloned.1.call-done = f32[512,256]{1,0:T(8,128)} async-done(((f32[4096,256]{1,0:T(8,128)}), f32[512,256]{1,0:T(8,128)}) %reduce-scatter.3.cloned.1.call-update) | async-done | bytes 524304 | tf_op jit(solution)/shard_map/reduce_scatter | solution.py:34
  102.4 0.0 copy-done.2
  102.4 2.2 multiply_convert_fusion
  104.6 0.0 all-gather.5.cloned.1.call-update
  104.6 0.0 reduce-scatter.5.cloned.1.call-start
  104.6 0.1 copy.45
  104.7 27.2 %all-gather.5.cloned.1.call-done = bf16[4096,256]{1,0:T(8,128)(2,1)} async-done(((bf16[512,256]{1,0:T(8,128)(2,1)}), bf16[4096,256]{1,0:T(8,128)(2,1)}) %all-gather.5.cloned.1.call-update) | async-done | bytes 2097168 | tf_op jit(solution)/shard_map/all_gather | solution.py:42
  132.0 8.5 %convolution_bitcast_fusion = f32[16,2,256,256]{2,3,1,0:T(8,128)} fusion(bf16[16,256,256,1]{2,1,3,0:T(8,128)(2,1)} %bitcast.39, s32[16,2,256,256]{3,2,1,0:T(8,128)} %param.8), kind=kOutput, calls=%fused_computation.6 | convolution fusion | flops 1075838976 | bytes 18874368 | tf_op jit(solution)/shard_map/bkij,bif->bkjf/dot_general | solution.py:45
  140.5 10.5 %copy.47 = f32[16,2,256,256]{3,0,1,2:T(8,128)} copy(f32[16,2,256,256]{2,3,1,0:T(8,128)} %convolution_bitcast_fusion) | data formatting | bytes 16777216 | tf_op jit(solution)/shard_map/bkij,bif->bkjf/dot_general | solution.py:45
  151.0 0.0 copy-done.3
  151.0 5.2 %convolution_bitcast_fusion.1 = f32[8,256,256]{2,0,1:T(8,128)S(1)} fusion(f32[16,2,256,256]{3,0,1,2:T(8,128)} %copy.47, s32[16,2]{0,1:T(2,128)S(1)} %copy-done.3, pred[16,2]{0,1:T(4,128)(4,1)S(1)} %copy.45), kind=kOutput, calls=%fused_computation.12 | convolution fusion | flops 201327104 | bytes 10485920 | tf_op jit(solution)/shard_map/bkc,bkjf->cjf/dot_general | solution.py:49
  156.3 0.0 copy-start.1
  156.3 2.0 copy.48
  158.2 0.0 reduce-scatter.5.cloned.1.call-update
  158.3 0.0 all-reduce.3.cloned.1.call-start
  158.3 34.8 %reduce-scatter.5.cloned.1.call-done = f32[512,256]{1,0:T(8,128)} async-done(((f32[2048,256]{1,0:T(8,128)}), f32[512,256]{1,0:T(8,128)}) %reduce-scatter.5.cloned.1.call-update) | async-done | bytes 524304 | tf_op jit(solution)/shard_map/reduce_scatter | solution.py:51
  193.1 0.0 copy-done.1
  193.1 2.0 convolution_bitcast_fusion.2
  195.1 0.0 all-reduce.3.cloned.1.call-update
  195.2 2.0 convolution_convert_fusion.1
  197.2 127.8 %all-reduce.3.cloned.1.call-done = f32[256,256]{0,1:T(8,128)} async-done(((f32[256,256]{0,1:T(8,128)}), f32[256,256]{0,1:T(8,128)}) %all-reduce.3.cloned.1.call-update) | async-done | bytes 262160 | tf_op jit(solution)/shard_map/psum | solution.py:59
  325.0 1.0 broadcast_multiply_fusion
  326.0 0.8 copy.49
  (4 shorter events, 0.0 us)
Async XLA Ops:
  7.2 32.1 %copy-start = (bf16[256,256]{1,0:T(8,128)(2,1)S(1)}, bf16[256,256]{1,0:T(8,128)(2,1)}, u32[]{:S(2)}) copy-start(bf16[256,256]{1,0:T(8,128)(2,1)} %param.7) | copy-start | bytes 393220
  7.2 32.0 %all-gather.3.cloned.1.call-start = ((), (), s32[]{:S(2)}) async-start(), calls=%async_computation.2 | async-start | bytes 1310720 | tf_op jit(solution)/shard_map/all_gather | solution.py:16
  7.9 94.5 %reduce-scatter.3.cloned.1.call-start = ((), (), s32[]{:S(2)}) async-start(), calls=%async_computation.3 | async-start | bytes 4718592 | tf_op jit(solution)/shard_map/reduce_scatter | solution.py:34
  51.6 80.4 %all-gather.5.cloned.1.call-start = ((), (), s32[]{:S(2)}) async-start(), calls=%async_computation.4 | async-start | bytes 2359296 | tf_op jit(solution)/shard_map/all_gather | solution.py:42
  51.7 4.8 %copy-start.4 = (u32[32]{0:T(128)S(1)}, u32[32]{0:T(128)}, u32[]{:S(2)}) copy-start(u32[32]{0:T(128)} %constant.31) | copy-start | bytes 388
  51.7 50.7 %copy-start.2 = (bf16[512,256]{1,0:T(8,128)(2,1)S(1)}, bf16[512,256]{1,0:T(8,128)(2,1)}, u32[]{:S(2)}) copy-start(bf16[512,256]{1,0:T(8,128)(2,1)} %param.11) | copy-start | bytes 786436
  104.6 88.5 %reduce-scatter.5.cloned.1.call-start = ((), (), s32[]{:S(2)}) async-start(), calls=%async_computation.5 | async-start | bytes 2621440 | tf_op jit(solution)/shard_map/reduce_scatter | solution.py:51
  140.5 10.5 %copy-start.3 = (s32[16,2]{0,1:T(2,128)S(1)}, s32[16,2]{0,1:T(2,128)}, u32[]{:S(2)}) copy-start(s32[16,2]{0,1:T(2,128)} %param.9) | copy-start | bytes 388
  156.3 36.9 %copy-start.1 = (bf16[512,256]{1,0:T(8,128)(2,1)S(1)}, bf16[512,256]{1,0:T(8,128)(2,1)}, u32[]{:S(2)}) copy-start(bf16[512,256]{1,0:T(8,128)(2,1)} %param.6) | copy-start | bytes 786436
  158.3 166.7 %all-reduce.3.cloned.1.call-start = ((), (), s32[]{:S(2)}) async-start(), calls=%async_computation.6 | async-start | bytes 524288 | tf_op jit(solution)/shard_map/psum | solution.py:59
Sparse Core Ops, SparseCore 0:
  9.9 29.3 all-gather.2
  51.7 50.6 reduce-scatter.2
  104.7 27.2 all-gather.4
  158.4 34.6 reduce-scatter.4
  199.9 124.9 all-reduce.2
where the time goes:
time: 334 us; the launch traced here: 333 us
  waiting for transfers between devices  234 us (70%)
  blocking collectives  30.4 us (9%)
  matrix products  27.4 us (8%)
  local copies, waits for them, and re-layouts  17.1 us (5%)
  between operations  14.6 us (4%)
  other arithmetic  10 us (3%)
    psum x1, waiting for transfers between devices, shards(): lax.psum(weight_terms, ('row', 'col'))  128 us
    reduce_scatter x1, waiting for transfers between devices, shards(): lax.psum_scatter(col_partial, 'row', scatter_dimension=0, tiled=True)  34.8 us
    unnamed x1, blocking collectives  30.4 us
    all_gather x1, waiting for transfers between devices, shards(): col_inputs = lax.all_gather(features, 'row', axis=0, tiled=True)  28.9 us
    all_gather x1, waiting for transfers between devices, shards(): lax.all_gather(grad_sum, 'col', axis=0, tiled=True)  27.2 us
    reduce_scatter x1, waiting for transfers between devices, shards(): lax.psum_scatter(partial_value, 'col', scatter_dimension=0, tiled=True)  14.2 us
    dot_general x1, local copies, waits for them, and re-layouts, shards(): jnp.einsum('bkij,bif->bkjf', tile_bf, grad_slab, preferred_element_type=j...  10.5 us
    dot_general x1, matrix products, shards(): jnp.einsum('bkij,bif->bkjf', tile_bf, grad_slab, preferred_element_type=j...  8.54 us
  transfers between devices with their start and end apart: 5, of which 5 were waited for; matrix products, arithmetic and copies ran while one was open for 3% of the time, Pallas kernels for 0%

commit v1 on v0

--- a/solution.py
+++ b/solution.py
@@ -56,7 +56,9 @@
     )
     node_total = own_rows * lax.axis_size("row") * lax.axis_size("col")
     weight_terms = jnp.dot(features.T, node_grad, preferred_element_type=jnp.float32)
-    weight_grad = lax.psum(weight_terms, ("row", "col")) * jnp.float32(1.0 / math.sqrt(node_total))
+    weight_grad = jnp.sum(lax.all_gather(weight_terms, ("row", "col")), axis=0) * jnp.float32(
+        1.0 / math.sqrt(node_total)
+    )
     return (output, feature_grad, weight_grad)
 
 

time: 334 us -> 298 us (0.89)
  waiting for transfers between devices: 234 us -> 190 us
  local copies, waits for them, and re-layouts: 17.1 us -> 23.9 us
    psum x1 -> x0, waiting for transfers between devices: 128 us -> none  [shards(): lax.psum(weight_terms, ('row', 'col'))]
    all_gather x0 -> x1, waiting for transfers between devices: none -> 84.3 us  [shards(): lax.all_gather(weight_terms, ('row', 'col'))]
    unnamed x13 -> x14, local copies, waits for them, and re-layouts: 1.46 us -> 8.3 us
where the time goes in v1:
time: 298 us
  waiting for transfers between devices  190 us (64%)
  blocking collectives  30.4 us (10%)
  matrix products  27.4 us (9%)
  local copies, waits for them, and re-layouts  23.9 us (8%)
  between operations  14.6 us (5%)
  other arithmetic  11 us (4%)
    all_gather x1, waiting for transfers between devices, shards(): lax.all_gather(weight_terms, ('row', 'col'))  84.3 us
    reduce_scatter x1, waiting for transfers between devices, shards(): lax.psum_scatter(col_partial, 'row', scatter_dimension=0, tiled=True)  34.6 us
    unnamed x1, blocking collectives  30.4 us
    all_gather x1, waiting for transfers between devices, shards(): col_inputs = lax.all_gather(features, 'row', axis=0, tiled=True)  28.9 us
    all_gather x1, waiting for transfers between devices, shards(): lax.all_gather(grad_sum, 'col', axis=0, tiled=True)  27.3 us
    reduce_scatter x1, waiting for transfers between devices, shards(): lax.psum_scatter(partial_value, 'col', scatter_dimension=0, tiled=True)  14.2 us
    dot_general x1, local copies, waits for them, and re-layouts, shards(): jnp.einsum('bkij,bif->bkjf', tile_bf, grad_slab, preferred_element_type=j...  10.5 us
    dot_general x1, matrix products, shards(): jnp.einsum('bkij,bif->bkjf', tile_bf, grad_slab, preferred_element_type=j...  8.54 us
  transfers between devices with their start and end apart: 5, of which 5 were waited for; matrix products, arithmetic and copies ran while one was open for 3% of the time, Pallas kernels for 0%

profile of v1, /device:TPU:0, one launch (start us, length us, event | category | flops | bytes accessed | tf_op | source)
XLA Modules:
  0.0 297.6 jit_solution(8800420176423291270)
XLA Ops:
  7.2 0.0 copy-start
  7.2 0.0 all-gather.5.cloned.1.call-start
  7.2 0.7 all-gather.5.cloned.1.call-update
  7.9 0.0 reduce-scatter.3.cloned.1.call-start
  8.0 0.7 compare_and_fusion
  8.6 0.1 copy.40
  8.7 0.7 compare_select_fusion
  9.4 0.1 copy.41
  9.5 0.1 reshape.78
  9.6 0.7 iota_compare_fusion.1
  10.4 28.9 %all-gather.5.cloned.1.call-done = bf16[2048,256]{1,0:T(8,128)(2,1)} async-done(((bf16[512,256]{1,0:T(8,128)(2,1)}), bf16[2048,256]{1,0:T(8,128)(2,1)}) %all-gather.5.cloned.1.call-update) | async-done | bytes 1048592 | tf_op jit(solution)/shard_map/all_gather | solution.py:16
  39.2 0.0 copy-done
  39.2 1.7 convolution_convert_fusion
  40.9 2.8 gather_fusion
  43.7 7.9 %fusion = f32[16,256,256,1]{1,2,3,0:T(8,128)} fusion(bf16[16,2,256,256]{3,2,1,0:T(8,128)(2,1)} %bitcast.41, pred[16,2]{1,0:T(8,128)(4,1)S(1)} %copy.40, pred[16,2]{1,0:T(8,128)(4,1)S(1)} %iota_compare_fusion.1, s32[16,2,256,256]{3,2,1,0:T(8,128)} %param.8), kind=kOutput, calls=%fused_computation.2 | convolution fusion | flops 1080033280 | bytes 16777280 | tf_op jit(solution)/shard_map/bkij,bkjf->bif/dot_general | solution.py:25
  51.6 0.0 reduce-scatter.3.cloned.1.call-update
  51.6 0.0 all-gather.7.cloned.1.call-start
  51.7 0.0 copy-start.4
  51.7 0.0 copy-start.2
  51.7 4.6 %reduce_sum.27 = s32[16,2,256]{2,1,0:T(2,128)S(1)} reduce(s32[16,2,256,256]{3,2,1,0:T(8,128)} %param.8, s32[]{:T(128)} %constant.8.clone.1), dimensions={3}, to_apply=%region_1.2 | reduce | flops 2088960 | bytes 8421380 | tf_op jit(solution)/shard_map/reduce_sum | solution.py:29
  56.3 0.1 select_reduce_fusion
  56.5 0.0 copy-done.4
  56.5 0.6 dynamic-slice
  57.7 30.4 %all-reduce = f32[4096]{0:T(1024)S(1)} all-reduce(f32[4096]{0:T(1024)S(1)} %bitcast.46), channel_id=4, replica_groups=mesh['row'=4,'col'=8] {'col'}, use_global_device_ids=true, to_apply=%region_3.4.clone | all-reduce | flops 4096 | bytes 32768
  88.1 0.1 fusion.16
  88.2 14.2 %reduce-scatter.3.cloned.1.call-done = f32[512,256]{1,0:T(8,128)} async-done(((f32[4096,256]{1,0:T(8,128)}), f32[512,256]{1,0:T(8,128)}) %reduce-scatter.3.cloned.1.call-update) | async-done | bytes 524304 | tf_op jit(solution)/shard_map/reduce_scatter | solution.py:34
  102.4 0.0 copy-done.2
  102.4 2.2 multiply_convert_fusion
  104.5 0.0 all-gather.7.cloned.1.call-update
  104.6 0.0 reduce-scatter.5.cloned.1.call-start
  104.6 0.1 copy.43
  104.7 27.3 %all-gather.7.cloned.1.call-done = bf16[4096,256]{1,0:T(8,128)(2,1)} async-done(((bf16[512,256]{1,0:T(8,128)(2,1)}), bf16[4096,256]{1,0:T(8,128)(2,1)}) %all-gather.7.cloned.1.call-update) | async-done | bytes 2097168 | tf_op jit(solution)/shard_map/all_gather | solution.py:42
  132.0 8.5 %convolution_bitcast_fusion = f32[16,2,256,256]{2,3,1,0:T(8,128)} fusion(bf16[16,256,256,1]{2,1,3,0:T(8,128)(2,1)} %bitcast.45, s32[16,2,256,256]{3,2,1,0:T(8,128)} %param.8), kind=kOutput, calls=%fused_computation.7 | convolution fusion | flops 1075838976 | bytes 18874368 | tf_op jit(solution)/shard_map/bkij,bif->bkjf/dot_general | solution.py:45
  140.5 10.5 %copy.45 = f32[16,2,256,256]{3,0,1,2:T(8,128)} copy(f32[16,2,256,256]{2,3,1,0:T(8,128)} %convolution_bitcast_fusion) | data formatting | bytes 16777216 | tf_op jit(solution)/shard_map/bkij,bif->bkjf/dot_general | solution.py:45
  151.0 0.0 copy-done.3
  151.0 5.2 %convolution_bitcast_fusion.1 = f32[8,256,256]{2,0,1:T(8,128)S(1)} fusion(f32[16,2,256,256]{3,0,1,2:T(8,128)} %copy.45, s32[16,2]{0,1:T(2,128)S(1)} %copy-done.3, pred[16,2]{0,1:T(4,128)(4,1)S(1)} %copy.43), kind=kOutput, calls=%fused_computation.13 | convolution fusion | flops 201327104 | bytes 10485920 | tf_op jit(solution)/shard_map/bkc,bkjf->cjf/dot_general | solution.py:49
  156.3 0.0 copy-start.1
  156.3 2.0 copy.46
  158.2 0.0 reduce-scatter.5.cloned.1.call-update
  158.3 0.2 all-gather.9.cloned.1.call-start
  158.5 34.6 %reduce-scatter.5.cloned.1.call-done = f32[512,256]{1,0:T(8,128)} async-done(((f32[2048,256]{1,0:T(8,128)}), f32[512,256]{1,0:T(8,128)}) %reduce-scatter.5.cloned.1.call-update) | async-done | bytes 524304 | tf_op jit(solution)/shard_map/reduce_scatter | solution.py:51
  193.1 2.0 convolution_bitcast_fusion.2
  195.1 0.0 all-gather.9.cloned.1.call-update
  195.2 2.0 convolution_convert_fusion.1
  197.2 84.3 %all-gather.9.cloned.1.call-done = f32[8192,256]{0,1:T(8,128)} async-done(((f32[256,256]{0,1:T(8,128)}), f32[8192,256]{0,1:T(8,128)}) %all-gather.9.cloned.1.call-update) | async-done | bytes 8388624 | tf_op jit(solution)/shard_map/all_gather | solution.py:59
  281.4 6.8 %copy.55 = f32[32,8,32,256]{3,2,1,0:T(8,128)S(1)} copy(f32[32,8,32,256]{3,1,2,0:T(8,128)} %bitcast.43) | data formatting | bytes 16777216
  288.3 1.9 bitcast_reduce_fusion
  290.2 0.8 copy.47
  (6 shorter events, 0.0 us)
Async XLA Ops:
  7.2 32.1 %copy-start = (bf16[256,256]{1,0:T(8,128)(2,1)S(1)}, bf16[256,256]{1,0:T(8,128)(2,1)}, u32[]{:S(2)}) copy-start(bf16[256,256]{1,0:T(8,128)(2,1)} %param.7) | copy-start | bytes 393220
  7.2 32.0 %all-gather.5.cloned.1.call-start = ((), (), s32[]{:S(2)}) async-start(), calls=%async_computation.2 | async-start | bytes 1310720 | tf_op jit(solution)/shard_map/all_gather | solution.py:16
  7.9 94.5 %reduce-scatter.3.cloned.1.call-start = ((), (), s32[]{:S(2)}) async-start(), calls=%async_computation.3 | async-start | bytes 4718592 | tf_op jit(solution)/shard_map/reduce_scatter | solution.py:34
  51.6 80.4 %all-gather.7.cloned.1.call-start = ((), (), s32[]{:S(2)}) async-start(), calls=%async_computation.4 | async-start | bytes 2359296 | tf_op jit(solution)/shard_map/all_gather | solution.py:42
  51.7 4.8 %copy-start.4 = (u32[32]{0:T(128)S(1)}, u32[32]{0:T(128)}, u32[]{:S(2)}) copy-start(u32[32]{0:T(128)} %constant.33) | copy-start | bytes 388
  51.7 50.7 %copy-start.2 = (bf16[512,256]{1,0:T(8,128)(2,1)S(1)}, bf16[512,256]{1,0:T(8,128)(2,1)}, u32[]{:S(2)}) copy-start(bf16[512,256]{1,0:T(8,128)(2,1)} %param.11) | copy-start | bytes 786436
  104.6 88.6 %reduce-scatter.5.cloned.1.call-start = ((), (), s32[]{:S(2)}) async-start(), calls=%async_computation.5 | async-start | bytes 2621440 | tf_op jit(solution)/shard_map/reduce_scatter | solution.py:51
  140.5 10.5 %copy-start.3 = (s32[16,2]{0,1:T(2,128)S(1)}, s32[16,2]{0,1:T(2,128)}, u32[]{:S(2)}) copy-start(s32[16,2]{0,1:T(2,128)} %param.9) | copy-start | bytes 388
  156.3 36.9 %copy-start.1 = (bf16[512,256]{1,0:T(8,128)(2,1)S(1)}, bf16[512,256]{1,0:T(8,128)(2,1)}, u32[]{:S(2)}) copy-start(bf16[512,256]{1,0:T(8,128)(2,1)} %param.6) | copy-start | bytes 786436
  158.3 123.2 %all-gather.9.cloned.1.call-start = ((), (), s32[]{:S(2)}) async-start(), calls=%async_computation.6 | async-start | bytes 8650752 | tf_op jit(solution)/shard_map/all_gather | solution.py:59
Sparse Core Ops, SparseCore 0:
  9.9 29.3 all-gather.4
  51.7 50.5 reduce-scatter.2
  104.7 27.2 all-gather.6
  158.4 34.6 reduce-scatter.4
  196.9 84.5 all-gather.8
